TPU v7x, 32 devices: a whole 2x2x4 slice. The times are simulated.
32 devices in a mesh: ga: 16 (over z, x, core), band: 2 (over y).
Axes of the slice: x: 2, y: 2, z: 4, core: 2. Of those that a mesh axis runs over, the one named last changes fastest.
Arguments:
- orbitals: bfloat16 [2, 2, 128, 192], P(None, None, ('ga', 'band')), may hold values from -6 to 6
- projectors: bfloat16 [512, 2, 128, 192], P(None, None, ('ga', 'band')), may hold values from -0.09375 to 0.09375
- potential: float32 [192, 192, 192], P('ga'), may hold values from -2 to 0.5
- couplings: float32 [512, 512], replicated, may hold values from -3 to 3
- atom_index: int32 [512], replicated, may hold values from 0 to 63
- column_site: int32 [128], replicated, may hold values from 0 to 36863, as said below
- column_count: int32 [16], replicated, may hold values from 2 to 8, as said below
Outputs:
- applied: float32 [2, 2, 128, 192], P(None, None, ('ga', 'band'))
Inputs may be any that keep to these rules, and one draw needn't show every extreme that they name: `column_site`: distinct positions kx * 192 + ky in the 192 x 192 plane of frequencies. `column_count`: the slot b * 4 + j of band index b in a ga block is used where it lies below that block's count; some ga block has all 8 slots used.
All inputs are finite; a program needn't handle non-finite values.
Results may differ from a plain program's by a relative error of at most 0.0027.
Values may be sent and summed in bfloat16 or wider, within the bound.
No kernel may reach another device: no remote copies, remote signals or barrier semaphores. Data moves between devices by JAX's collectives and lax.ppermute only.
A program may use at most 128 MiB of HBM per device.

v0:
```python
import functools

import jax
import jax.numpy as jnp
import ml_dtypes
import numpy as np
from jax import lax
from jax.experimental import pallas as pl
from jax.experimental.pallas import tpu as pltpu
from jax.sharding import PartitionSpec as P

LANES = 128
BF16 = jnp.bfloat16
F32 = jnp.float32


def pieces_of(table):
    table = np.asarray(table, np.float32)
    head = table.astype(ml_dtypes.bfloat16)
    return np.stack([head, (table - head.astype(np.float32)).astype(ml_dtypes.bfloat16)])


def line_table(length, blocks, planes, width):
    kz = np.arange(length)
    out = np.zeros((2, length, blocks, width), np.float64)
    for block in range(blocks):
        z = block * planes + np.arange(planes)
        phases = (kz[:, None] * z[None, :] % length) * (2.0 * np.pi / length)
        out[0, :, block, :planes] = np.cos(phases)
        out[0, :, block, width // 2 : width // 2 + planes] = np.sin(phases)
        out[1, :, block, :planes] = -np.sin(phases)
        out[1, :, block, width // 2 : width // 2 + planes] = np.cos(phases)
    return pieces_of(out.reshape(2, length, blocks * width))


def split(values):
    head = values.astype(BF16)
    return head, (values - head.astype(F32)).astype(BF16)


def stacked(values):
    head, rest = split(values)
    return jnp.concatenate([head.astype(F32), rest.astype(F32)], axis=0).astype(BF16)


def both_pieces(values):
    return jnp.concatenate(split(values), axis=1)


def dot(left, right):
    return lax.dot_general(left, right, (((1,), (0,)), ((), ())), preferred_element_type=F32)


def dot_nt(left, right):
    return lax.dot_general(left, right, (((1,), (1,)), ((), ())), preferred_element_type=F32)


def lane_ids(rows):
    return lax.broadcasted_iota(jnp.int32, (rows, LANES), 1)


def used_slots(count_ref, slots):
    used = count_ref[lax.axis_index("ga")] - lax.axis_index("band") * slots
    return lax.broadcasted_iota(jnp.int32, (slots, 1), 0) < used


def cosine_and_sine(phases, length):
    quarter = jnp.floor(phases * (4.0 / length) + 0.5)
    angle = (phases - quarter * (length / 4.0)) * (2.0 * np.pi / length)
    square = angle * angle
    sine = 1.0 / 362880.0
    for term in (-1.0 / 5040.0, 1.0 / 120.0, -1.0 / 6.0, 1.0):
        sine = sine * square + term
    sine = sine * angle
    cosine = -1.0 / 3628800.0
    for term in (1.0 / 40320.0, -1.0 / 720.0, 1.0 / 24.0, -0.5, 1.0):
        cosine = cosine * square + term
    quarter = quarter - 4.0 * jnp.floor(quarter * 0.25)
    odd = (quarter == 1.0) | (quarter == 3.0)
    first = jnp.where(odd, sine, cosine)
    second = jnp.where(odd, cosine, sine)
    first = jnp.where((quarter == 1.0) | (quarter == 2.0), -first, first)
    return first, jnp.where(quarter >= 2.0, -second, second)


def project_kernel(sizes, count_hbm, orbitals_hbm, projectors_hbm, out_ref, *scratch):
    blocks, groups, orbitals, slots, length, projectors, planes, width = sizes
    count_ref, orbitals_ref, projectors_ref, coef, lines, small_sems, sems = scratch
    kinds = orbitals * 2
    devices = blocks * groups
    share = projectors // devices
    small = [
        pltpu.make_async_copy(count_hbm, count_ref, small_sems.at[0]),
        pltpu.make_async_copy(orbitals_hbm, orbitals_ref, small_sems.at[1]),
    ]
    copies = []
    for piece in range(2 * slots):
        rows = pl.ds(piece * length, length)
        copies.append(pltpu.make_async_copy(projectors_hbm.at[rows], projectors_ref.at[rows], sems.at[piece]))
    for copy in small + copies:
        copy.start()
    half = width // 2
    lanes = lax.broadcasted_iota(jnp.int32, (length, blocks * half), 1)
    plane = (lanes >> (half.bit_length() - 1)) * planes + (lanes & (half - 1))
    kz = lax.broadcasted_iota(jnp.int32, (length, blocks * half), 0)
    table = split(jnp.concatenate(cosine_and_sine(kz.astype(F32) * plane.astype(F32), length), axis=1))
    coef[...] = jnp.zeros_like(coef)
    small[0].wait()
    small[1].wait()
    used = used_slots(count_ref, slots)
    for n in range(orbitals):
        for part in range(2):
            values = jnp.where(used, orbitals_ref[n, part].astype(F32), 0.0)
            at = (part * orbitals + n) * slots
            lines[at : at + slots, :] = values
            turned = values if part == 1 else -values
            for slot in range(slots):
                row = n * 2 + part
                coef[slot, row : row + 1, :] = values[slot : slot + 1, :]
                row = n * 2 + 1 - part
                coef[slots + slot, row : row + 1, :] = turned[slot : slot + 1, :]
    left = lines[...].astype(BF16)
    both = dot(left, table[0]) + dot(left, table[1])
    rows = orbitals * slots
    points = blocks * half
    real = both[:rows, :points] - both[rows:, points:]
    imag = both[:rows, points:] + both[rows:, :points]
    lanes = lane_ids(rows)
    rows_each = slots // 2
    piece_lanes = lane_ids(rows_each)
    for block in range(blocks):
        at = block * half
        base = at // LANES * LANES
        chunk = pltpu.roll(imag[:, base : base + LANES], (base - at + half) % LANES, 1)
        chunk = jnp.where(lanes < half, pltpu.roll(real[:, base : base + LANES], (base - at) % LANES, 1), chunk)
        aside = pltpu.roll(chunk, width, 1)
        for group in range(groups):
            at = group * slots
            piece = jnp.where(piece_lanes < width, chunk[at : at + rows_each, :], aside[at + rows_each : at + slots, :])
            out_ref[block * groups + group] = piece
    sums = jnp.zeros((coef.shape[1], projectors), F32)
    for piece in range(2 * slots):
        left = coef[piece].astype(BF16)
        copies[piece].wait()
        sums += dot(left, projectors_ref[piece * length : (piece + 1) * length, :])
    for device in range(devices):
        piece = jnp.where(piece_lanes < 2 * width, out_ref[device], 0.0)
        first = device * share
        base = first // LANES * LANES
        for group in range(kinds // rows_each):
            low = 2 * width + group * share
            own = sums[group * rows_each : (group + 1) * rows_each, base : base + LANES]
            own = pltpu.roll(own, (base + low - first) % LANES, 1)
            piece = jnp.where((piece_lanes >= low) & (piece_lanes < low + share), own, piece)
        out_ref[device] = piece


def table_kernel(length, wide, slots, site_ref, x_ref, plus_ref):
    columns = site_ref.shape[1]
    each = slots // 2
    eye = lax.broadcasted_iota(jnp.int32, (LANES, LANES), 0) == lane_ids(LANES)
    row_ids = lax.broadcasted_iota(jnp.int32, (length, LANES), 0).astype(F32)
    lanes = lax.broadcasted_iota(jnp.int32, (LANES, wide), 1)
    inside = lanes < length
    lanes = lanes.astype(F32)
    sites = site_ref[...].astype(F32)
    stored = lax.broadcasted_iota(jnp.int32, (LANES, columns), 1)
    for at in range(0, columns, LANES):
        order = lax.broadcasted_iota(jnp.int32, (LANES, columns), 0) + at
        second = order >= columns // 2
        order = jnp.where(second, order - columns // 2, order)
        wanted = (order >> (each.bit_length() - 1)) * slots + (order & (each - 1)) + jnp.where(second, each, 0)
        along = jnp.sum(jnp.where(stored == wanted, sites, 0.0), axis=1, keepdims=True)
        site = jnp.sum(jnp.where(eye, along, 0.0), axis=0, keepdims=True)
        site_x = jnp.floor((site + 0.5) * (1.0 / length))
        along = along - jnp.floor((along + 0.5) * (1.0 / length)) * length
        cosine, sine = cosine_and_sine(row_ids * site_x, length)
        x_ref[:, at : at + LANES] = cosine
        x_ref[:, columns + at : columns + at + LANES] = sine
        cosine, sine = cosine_and_sine(lanes * along, length)
        cosine = jnp.where(inside, cosine, 0.0)
        sine = jnp.where(inside, sine, 0.0)
        cosine = cosine.astype(BF16)
        sine = sine.astype(BF16)
        for piece in range(2):
            rows = pl.ds(piece * 2 * columns + at, LANES)
            plus_ref[rows, :wide] = cosine
            plus_ref[rows, wide:] = sine
            rows = pl.ds((piece * 2 + 1) * columns + at, LANES)
            plus_ref[rows, :wide] = -sine
            plus_ref[rows, wide:] = cosine


def plane_kernel(sizes, columns_ref, x_ref, plus_ref, potential_ref, out_ref, gathered, lines, back, turning):
    devices, slots, planes, length, wide, width, carried, batch = sizes
    count = devices * slots
    each = slots // 2
    middle = count // 2
    total = jnp.zeros((each, LANES), F32)
    for device in range(devices):
        piece = columns_ref[device]
        gathered[device * each : (device + 1) * each, :] = piece
        total += piece
    for at in range(0, middle, LANES):
        size = min(LANES, middle - at)
        turned = gathered[at : at + LANES, :].T
        for side in range(2):
            lines[:, side * middle + at : side * middle + at + size] = turned[side * width : (side + 1) * width, :size]
    back[...] = jnp.zeros_like(back)
    cosine = x_ref[:, :count]
    sine = x_ref[:, count:]
    padding = jnp.zeros((length, wide - length), F32)
    for i in range(planes // batch):
        left = []
        for plane in range(i * batch, (i + 1) * batch):
            real = lines[plane : plane + 1, :]
            imag = lines[plane + width // 2 : plane + width // 2 + 1, :]
            left.append(jnp.concatenate([cosine * real - sine * imag, cosine * imag + sine * real], axis=1))
        left = both_pieces(jnp.concatenate(left, axis=0))
        field = dot(left, plus_ref[...])
        weights = []
        for plane in range(i * batch, (i + 1) * batch):
            own = jnp.concatenate([potential_ref[plane], padding], axis=1)
            weights.append(jnp.concatenate([own, own], axis=1))
        left = (field * jnp.concatenate(weights, axis=0)).astype(BF16)
        half = dot_nt(left, plus_ref[: 2 * count, :])
        for j in range(batch):
            plane = i * batch + j
            real = half[j * length : (j + 1) * length, :count]
            imag = half[j * length : (j + 1) * length, count:]
            back[plane : plane + 1, :] = jnp.sum(cosine * real + sine * imag, axis=0, keepdims=True)
            at = plane + width // 2
            back[at : at + 1, :] = jnp.sum(cosine * imag - sine * real, axis=0, keepdims=True)
    for at in range(0, middle, LANES):
        size = min(LANES, middle - at)
        for side in range(2):
            turning[side * width : (side + 1) * width, :size] = back[:, side * middle + at : side * middle + at + size]
        gathered[at : at + LANES, :] = turning[...].T
    lanes = lane_ids(each)
    for device in range(devices):
        piece = gathered[device * each : (device + 1) * each, :]
        out_ref[device] = jnp.where((lanes >= 2 * width) & (lanes < carried), total, piece)


def finish_kernel(
    sizes, count_ref, columns_ref, atom_ref, couplings_ref, projectors_ref, table_ref, out_ref, summed, lined, mixed
):
    blocks, groups, orbitals, slots, length, projectors, width, normalizer = sizes
    kinds = orbitals * 2
    devices = blocks * groups
    share = projectors // devices
    each = slots // 2
    lanes = lane_ids(each)
    for chunk in range(projectors // LANES):
        in_chunk = range(chunk * LANES // share, (chunk + 1) * LANES // share)
        for rows in range(kinds // each):
            low = 2 * width + rows * share
            total = jnp.zeros((each, LANES), F32)
            for device in in_chunk:
                own = columns_ref[device]
                own = pltpu.roll(jnp.where((lanes >= low) & (lanes < low + share), own, 0.0), (device * share - low) % LANES, 1)
                total += own
            summed[rows * each : (rows + 1) * each, chunk * LANES : (chunk + 1) * LANES] = total
    for n in range(orbitals):
        at = kinds + n * 2
        summed[at : at + 1, :] = -summed[n * 2 + 1 : n * 2 + 2, :]
        summed[at + 1 : at + 2, :] = summed[n * 2 : n * 2 + 1, :]
    both = stacked(summed[...])
    atoms = atom_ref[...].astype(F32)
    eye = lax.broadcasted_iota(jnp.int32, (LANES, LANES), 0) == lane_ids(LANES)
    along = []
    for at in range(0, projectors, LANES):
        along.append(jnp.sum(jnp.where(eye, atoms[:, at : at + LANES], 0.0), axis=1, keepdims=True))
    head, rest = split(jnp.where(jnp.concatenate(along, axis=0) == atoms, couplings_ref[...], 0.0))
    head = dot_nt(both, head)
    rest = dot_nt(both, rest)
    weighted = (head[: 2 * kinds] + (head[2 * kinds :] + rest[: 2 * kinds])).astype(BF16)
    for slot in range(slots):
        rows = projectors_ref[slot * length : (slot + 1) * length, :]
        value = dot_nt(weighted, rows)[:kinds]
        rows = projectors_ref[(slots + slot) * length : (slots + slot + 1) * length, :]
        value = value + dot_nt(weighted, rows)[kinds:]
        for row in range(kinds):
            mixed[row, slot : slot + 1, :] = value[row : row + 1, :]
    for chunk in range(blocks * width // LANES):
        for group in range(groups):
            for side in range(2):
                low = side * width
                total = jnp.zeros((each, LANES), F32)
                for inner in range(LANES // width):
                    block = chunk * (LANES // width) + inner
                    own = columns_ref[block * groups + group]
                    own = jnp.where((lanes >= low) & (lanes < low + width), own, 0.0)
                    total += pltpu.roll(own, (inner * width - low) % LANES, 1)
                at = group * slots + side * each
                lined[at : at + each, chunk * LANES : (chunk + 1) * LANES] = total
    both = stacked(lined[...])
    rows_of_lines = groups * slots
    held = lax.broadcasted_iota(jnp.int32, (1, blocks), 1) == lax.axis_index("ga")
    used = jnp.sum(jnp.where(held, count_ref[...], 0).astype(F32), axis=1, keepdims=True)
    slot_ids = lax.broadcasted_iota(jnp.int32, (slots, 1), 0) + lax.axis_index("band") * slots
    used = slot_ids.astype(F32) < used
    for part in range(2):
        head = dot_nt(both, table_ref[0, part])
        rest = dot_nt(both, table_ref[1, part])
        local = (head[:rows_of_lines] + (head[rows_of_lines:] + rest[:rows_of_lines])) * normalizer
        for n in range(orbitals):
            value = local[n * slots : (n + 1) * slots, :] + mixed[n * 2 + part]
            out_ref[n, part] = jnp.where(used, value, 0.0)


def on_device(orbitals, projectors, potential, couplings, atom_index, column_site, column_count):
    blocks = lax.axis_size("ga")
    groups = lax.axis_size("band")
    devices = blocks * groups
    orbital_count, _, slots, length = orbitals.shape
    planes = potential.shape[0]
    projector_count = projectors.shape[0]
    columns = column_site.shape[0]
    kinds = orbital_count * 2
    assert orbital_count == groups and slots % 2 == 0 and kinds % (slots // 2) == 0 and columns % LANES == 0
    share = projector_count // devices
    width = 2
    while width < 2 * planes:
        width *= 2
    carried = 2 * width + kinds // (slots // 2) * share
    assert carried <= LANES and width <= LANES and share * devices == projector_count
    wide = -(-length // LANES) * LANES
    flat = jnp.transpose(projectors, (1, 2, 3, 0)).reshape(2 * slots * length, projector_count)
    z_table = line_table(length, blocks, planes, width)
    batch = next(i for i in (2, 3, 1) if planes % i == 0) if columns <= 512 else 1
    vmem = pl.BlockSpec(memory_space=pltpu.VMEM)
    hbm = pl.BlockSpec(memory_space=pltpu.HBM)
    params = pltpu.CompilerParams(vmem_limit_bytes=56 * 1024 * 1024)
    small = pltpu.CompilerParams(vmem_limit_bytes=40 * 1024 * 1024)
    payload = jax.ShapeDtypeStruct((devices, slots // 2, LANES), F32)

    sent = pl.pallas_call(
        functools.partial(
            project_kernel,
                (blocks, groups, orbital_count, slots, length, projector_count, planes, width),
        ),
        out_shape=payload,
        in_specs=[hbm] * 3,
        out_specs=vmem,
        scratch_shapes=[
            pltpu.SMEM(column_count.shape, jnp.int32),
            pltpu.VMEM(orbitals.shape, BF16),
            pltpu.VMEM(flat.shape, BF16),
            pltpu.VMEM((2 * slots, -(-kinds // 8) * 8, length), F32),
            pltpu.VMEM((kinds * slots, length), F32),
            pltpu.SemaphoreType.DMA((2,)),
            pltpu.SemaphoreType.DMA((2 * slots,)),
        ],
        compiler_params=params,
        cost_estimate=pl.CostEstimate(
            flops=2 * flat.size * LANES * slots,
            bytes_accessed=2 * (flat.size + z_table.size + orbitals.size) + 4 * payload.size,
            transcendentals=length * blocks * width,
        ),
        name="project",
    )(column_count, orbitals, flat)
    arrived = lax.all_to_all(sent, ("ga", "band"), split_axis=0, concat_axis=0, tiled=True)

    x_rows, plus = pl.pallas_call(
        functools.partial(table_kernel, length, wide, slots),
        out_shape=(
            jax.ShapeDtypeStruct((length, 2 * columns), F32),
            jax.ShapeDtypeStruct((4 * columns, 2 * wide), BF16),
        ),
        in_specs=[vmem],
        out_specs=(vmem,) * 2,
        compiler_params=small,
        cost_estimate=pl.CostEstimate(
            flops=4096 * potential.size,
            bytes_accessed=8 * (length + 2 * wide) * columns,
            transcendentals=2 * (length + wide) * columns,
        ),
        name="tables",
    )(column_site.reshape(1, columns))

    sent = pl.pallas_call(
        functools.partial(plane_kernel, (devices, slots, planes, length, wide, width, carried, batch)),
        out_shape=payload,
        in_specs=[vmem] * 4,
        out_specs=vmem,
        scratch_shapes=[
            pltpu.VMEM((-(-columns // (2 * LANES)) * LANES, LANES), F32),
            pltpu.VMEM((width, columns), F32),
            pltpu.VMEM((width, columns), F32),
            pltpu.VMEM((LANES, LANES), F32),
        ],
        compiler_params=small,
        cost_estimate=pl.CostEstimate(
            flops=12 * planes * length * wide * 2 * columns,
            bytes_accessed=4 * (potential.size + 2 * payload.size),
            transcendentals=0,
        ),
        name="planes",
    )(arrived, x_rows, plus, potential)
    arrived = lax.all_to_all(sent, ("ga", "band"), split_axis=0, concat_axis=0, tiled=True)

    normalizer = 1.0 / float(length**3)
    return pl.pallas_call(
        functools.partial(
            finish_kernel,
            (blocks, groups, orbital_count, slots, length, projector_count, width, normalizer),
        ),
        out_shape=jax.ShapeDtypeStruct(orbitals.shape, F32),
        in_specs=[vmem] * 6,
        out_specs=vmem,
        scratch_shapes=[
            pltpu.VMEM((2 * kinds, projector_count), F32),
            pltpu.VMEM((groups * slots, blocks * width), F32),
            pltpu.VMEM((kinds, slots, length), F32),
        ],
        compiler_params=small,
        cost_estimate=pl.CostEstimate(
            flops=4 * kinds * (4 * couplings.size + flat.size) + 4 * z_table.size * orbital_count * slots,
            bytes_accessed=4 * couplings.size + 2 * (flat.size + z_table.size) + 4 * orbitals.size,
            transcendentals=0,
        ),
        name="finish",
    )(column_count.reshape(1, blocks), arrived, atom_index.reshape(1, projector_count), couplings, flat, z_table)


def solution(mesh):
    return jax.shard_map(
        on_device,
        mesh=mesh,
        in_specs=(
            P(None, None, ("ga", "band"), None),
            P(None, None, ("ga", "band"), None),
            P("ga", None, None),
            P(),
            P(),
            P(),
            P(),
        ),
        out_specs=P(None, None, ("ga", "band"), None),
        check_vma=False,
    )
```

profile of v0, /device:TPU:0, one launch (start us, length us, event | category | flops | bytes accessed | tf_op | source)
XLA Modules:
  0.0 31.2 jit_solution(3552975188966590217)
XLA Ops:
  0.0 0.0 copy-start.6
  0.0 2.7 %project.1 = f32[32,2,128]{2,1,0:T(2,128)} custom-call(s32[16]{0:T(128)} %count_hbm.1, bf16[2,2,4,192]{3,2,1,0:T(4,128)(2,1)} %orbitals_hbm.1, bf16[1536,512]{1,0:T(8,128)(2,1)} %bitcast.6), custom_call_target="tpu_custom_call" | custom-call | flops 805306368 | bytes 2398208 | tf_op jit(solution)/shard_map/project/pallas_call | solution.py:338
  2.7 7.3 %all-to-all-start = ((f32[32,2,128]{2,1,0:T(2,128)}), f32[32,2,128]{2,1,0:T(2,128)S(1)}, u32[]{:S(2)}, u32[]{:S(2)}) async-start(f32[32,2,128]{2,1,0:T(2,128)} %project.1), calls=%async_computation | async-start | bytes 65536 | tf_op jit(solution)/shard_map/all_to_all | solution.py:363
  10.0 0.0 copy-done.6
  10.1 0.0 copy-start.5
  10.1 0.5 %tables.1 = (f32[192,256]{1,0:T(8,128)S(1)}, bf16[512,512]{1,0:T(8,128)(2,1)S(1)}) custom-call(s32[1,128]{1,0:T(1,128)S(1)} %bitcast.10), custom_call_target="tpu_custom_call" | custom-call | flops 1811939328 | bytes 720896 | tf_op jit(solution)/shard_map/tables/pallas_call | solution.py:365
  10.6 6.8 %all-to-all-done.columns_ref = f32[32,2,128]{2,1,0:T(2,128)S(1)} async-done(((f32[32,2,128]{2,1,0:T(2,128)}), f32[32,2,128]{2,1,0:T(2,128)S(1)}, u32[]{:S(2)}, u32[]{:S(2)}) %all-to-all-start) | async-done | bytes 32800 | tf_op jit(solution)/shard_map/all_to_all | solution.py:363
  17.4 0.0 copy-done.5
  17.4 0.0 copy-start
  17.4 0.0 copy-start.1
  17.4 0.0 copy-start.2
  17.4 0.0 copy-start.3
  17.4 0.0 copy-start.4
  17.4 2.7 %planes.1 = f32[32,2,128]{2,1,0:T(2,128)S(1)} custom-call(f32[32,2,128]{2,1,0:T(2,128)S(1)} %all-to-all-done.columns_ref, f32[192,256]{1,0:T(8,128)S(1)} %get-tuple-element.7.x_ref, bf16[512,512]{1,0:T(8,128)(2,1)S(1)} %get-tuple-element.8.plus_ref, f32[12,192,192]{2,1,0:T(8,128)S(1)} %copy-done.5), custom_call_target="tpu_custom_call" | custom-call | flops 1811939328 | bytes 1835008 | tf_op jit(solution)/shard_map/planes/pallas_call | solution.py:382
  20.1 9.0 %all_to_all.10.columns_ref = f32[32,2,128]{2,1,0:T(2,128)S(1)} all-to-all(f32[32,2,128]{2,1,0:T(2,128)S(1)} %planes.1), channel_id=1, replica_groups=mesh['ga'=16,'band'=2] {'ga','band'}, dimensions={0} | all-to-all | bytes 65536 | tf_op jit(solution)/shard_map/all_to_all | solution.py:401
  29.1 0.0 copy-done
  29.1 0.0 copy-done.1
  29.1 0.0 copy-done.2
  29.2 0.0 copy-done.3
  29.2 0.0 copy-done.4
  29.2 2.0 %finish.1 = f32[2,2,4,192]{3,2,1,0:T(4,128)} custom-call(s32[1,16]{1,0:T(1,128)S(1)} %bitcast.9, f32[32,2,128]{2,1,0:T(2,128)S(1)} %all_to_all.10.columns_ref, s32[1,512]{1,0:T(1,128)S(1)} %bitcast.8, f32[512,512]{1,0:T(8,128)S(1)} %copy-done.1, bf16[1536,512]{1,0:T(8,128)(2,1)S(1)} %bitcast.7, bf16[2,2,192,512]{3,2,1,0:T(8,128)(2,1)S(1)} %copy-done.2), custom_call_target="tpu_custom_call" | custom-call | flops 41943040 | bytes 3420160 | tf_op jit(solution)/shard_map/finish/pallas_call | solution.py:404
Async XLA Ops:
  0.0 10.1 %copy-start.6 = (s32[128]{0:T(128)S(1)}, s32[128]{0:T(128)}, u32[]{:S(2)}) copy-start(s32[128]{0:T(128)} %param.13) | copy-start | bytes 1540
  2.7 14.6 %all-to-all-start = ((f32[32,2,128]{2,1,0:T(2,128)}), f32[32,2,128]{2,1,0:T(2,128)S(1)}, u32[]{:S(2)}, u32[]{:S(2)}) async-start(f32[32,2,128]{2,1,0:T(2,128)} %project.1), calls=%async_computation | async-start | bytes 65536 | tf_op jit(solution)/shard_map/all_to_all | solution.py:363
  10.1 7.3 %copy-start.5 = (f32[12,192,192]{2,1,0:T(8,128)S(1)}, f32[12,192,192]{2,1,0:T(8,128)}, u32[]{:S(2)}) copy-start(f32[12,192,192]{2,1,0:T(8,128)} %potential_ref.1) | copy-start | bytes 5308420
  17.4 11.8 %copy-start = (bf16[512,2,4,192]{0,3,2,1:T(8,128)(2,1)S(1)}, bf16[512,2,4,192]{0,3,2,1:T(8,128)(2,1)}, u32[]{:S(2)}) copy-start(bf16[512,2,4,192]{0,3,2,1:T(8,128)(2,1)} %param.9) | copy-start | bytes 4718596
  17.4 11.8 %copy-start.1 = (f32[512,512]{1,0:T(8,128)S(1)}, f32[512,512]{1,0:T(8,128)}, u32[]{:S(2)}) copy-start(f32[512,512]{1,0:T(8,128)} %couplings_ref.1) | copy-start | bytes 3145732
  17.4 11.8 %copy-start.2 = (bf16[2,2,192,512]{3,2,1,0:T(8,128)(2,1)S(1)}, bf16[2,2,192,512]{3,2,1,0:T(8,128)(2,1)}, u32[]{:S(2)}) copy-start(bf16[2,2,192,512]{3,2,1,0:T(8,128)(2,1)} %constant.2.clone.table_ref) | copy-start | bytes 2359300
  17.4 11.8 %copy-start.3 = (s32[512]{0:T(512)S(1)}, s32[512]{0:T(512)}, u32[]{:S(2)}) copy-start(s32[512]{0:T(512)} %param.12) | copy-start | bytes 6148
  17.4 11.7 %copy-start.4 = (s32[16]{0:T(128)S(1)}, s32[16]{0:T(128)}, u32[]{:S(2)}) copy-start(s32[16]{0:T(128)} %count_hbm.1) | copy-start | bytes 196
where the time goes:
time: 31.4 us; the launch traced here: 31.2 us
  blocking collectives  9.04 us (29%)
  Pallas kernels  7.95 us (25%)
  starting transfers between devices  7.3 us (23%)
  waiting for transfers between devices  6.79 us (22%)
    all_to_all x1, blocking collectives, on_device(): lax.all_to_all(sent, ('ga', 'band'), split_axis=0, concat_axis=0, tiled=T...  9.04 us
    all_to_all x1, starting transfers between devices, on_device(): lax.all_to_all(sent, ('ga', 'band'), split_axis=0, concat_axis=0, tiled=T...  7.3 us
    all_to_all x1, waiting for transfers between devices, on_device(): lax.all_to_all(sent, ('ga', 'band'), split_axis=0, concat_axis=0, tiled=T...  6.79 us
    pallas_call x1, Pallas kernels, on_device(): pl.pallas_call(functools.partial(project_kernel, (blocks, groups, orbital...  2.73 us
    pallas_call x1, Pallas kernels, on_device(): pl.pallas_call(functools.partial(plane_kernel, (devices, slots, planes, l...  2.67 us
    pallas_call x1, Pallas kernels, on_device(): pl.pallas_call(functools.partial(finish_kernel, (blocks, groups, orbital_...  2.04 us
  transfers between devices with their start and end apart: 1, of which 1 were waited for; matrix products, arithmetic and copies ran while one was open for 0% of the time, Pallas kernels for 2%

commit v1 on v0

--- a/solution.py
+++ b/solution.py
@@ -328,7 +328,7 @@
     wide = -(-length // LANES) * LANES
     flat = jnp.transpose(projectors, (1, 2, 3, 0)).reshape(2 * slots * length, projector_count)
     z_table = line_table(length, blocks, planes, width)
-    batch = next(i for i in (2, 3, 1) if planes % i == 0) if columns <= 512 else 1
+    batch = next(i for i in (1,) if planes % i == 0) if columns <= 512 else 1
     vmem = pl.BlockSpec(memory_space=pltpu.VMEM)
     hbm = pl.BlockSpec(memory_space=pltpu.HBM)
     params = pltpu.CompilerParams(vmem_limit_bytes=56 * 1024 * 1024)

time: 31.4 us -> 32.2 us (1.025)
  Pallas kernels: 7.95 us -> 8.75 us
    pallas_call x1, Pallas kernels: 2.67 us -> 3.46 us  [on_device(): pl.pallas_call(functools.partial(plane_kernel, (devices, slots, planes, l...]
where the time goes in v1:
time: 32.2 us; the launch traced here: 32 us
  blocking collectives  9.04 us (28%)
  Pallas kernels  8.75 us (27%)
  starting transfers between devices  7.3 us (23%)
  waiting for transfers between devices  6.79 us (21%)
    all_to_all x1, blocking collectives, on_device(): lax.all_to_all(sent, ('ga', 'band'), split_axis=0, concat_axis=0, tiled=T...  9.04 us
    all_to_all x1, starting transfers between devices, on_device(): lax.all_to_all(sent, ('ga', 'band'), split_axis=0, concat_axis=0, tiled=T...  7.3 us
    all_to_all x1, waiting for transfers between devices, on_device(): lax.all_to_all(sent, ('ga', 'band'), split_axis=0, concat_axis=0, tiled=T...  6.79 us
    pallas_call x1, Pallas kernels, on_device(): pl.pallas_call(functools.partial(plane_kernel, (devices, slots, planes, l...  3.46 us
    pallas_call x1, Pallas kernels, on_device(): pl.pallas_call(functools.partial(project_kernel, (blocks, groups, orbital...  2.73 us
    pallas_call x1, Pallas kernels, on_device(): pl.pallas_call(functools.partial(finish_kernel, (blocks, groups, orbital_...  2.04 us
  transfers between devices with their start and end apart: 1, of which 1 were waited for; matrix products, arithmetic and copies ran while one was open for 0% of the time, Pallas kernels for 2%

profile of v1, /device:TPU:0, one launch (start us, length us, event | category | flops | bytes accessed | tf_op | source)
XLA Modules:
  0.0 32.0 jit_solution(7741994628213089343)
XLA Ops:
  0.0 0.0 copy-start.6
  0.0 2.7 %project.1 = f32[32,2,128]{2,1,0:T(2,128)} custom-call(s32[16]{0:T(128)} %count_hbm.1, bf16[2,2,4,192]{3,2,1,0:T(4,128)(2,1)} %orbitals_hbm.1, bf16[1536,512]{1,0:T(8,128)(2,1)} %bitcast.6), custom_call_target="tpu_custom_call" | custom-call | flops 805306368 | bytes 2398208 | tf_op jit(solution)/shard_map/project/pallas_call | solution.py:338
  2.7 7.3 %all-to-all-start = ((f32[32,2,128]{2,1,0:T(2,128)}), f32[32,2,128]{2,1,0:T(2,128)S(1)}, u32[]{:S(2)}, u32[]{:S(2)}) async-start(f32[32,2,128]{2,1,0:T(2,128)} %project.1), calls=%async_computation | async-start | bytes 65536 | tf_op jit(solution)/shard_map/all_to_all | solution.py:363
  10.0 0.0 copy-done.6
  10.1 0.0 copy-start.5
  10.1 0.5 %tables.1 = (f32[192,256]{1,0:T(8,128)S(1)}, bf16[512,512]{1,0:T(8,128)(2,1)S(1)}) custom-call(s32[1,128]{1,0:T(1,128)S(1)} %bitcast.10), custom_call_target="tpu_custom_call" | custom-call | flops 1811939328 | bytes 720896 | tf_op jit(solution)/shard_map/tables/pallas_call | solution.py:365
  10.6 6.8 %all-to-all-done.columns_ref = f32[32,2,128]{2,1,0:T(2,128)S(1)} async-done(((f32[32,2,128]{2,1,0:T(2,128)}), f32[32,2,128]{2,1,0:T(2,128)S(1)}, u32[]{:S(2)}, u32[]{:S(2)}) %all-to-all-start) | async-done | bytes 32800 | tf_op jit(solution)/shard_map/all_to_all | solution.py:363
  17.4 0.0 copy-done.5
  17.4 0.0 copy-start
  17.4 0.0 copy-start.1
  17.4 0.0 copy-start.2
  17.4 0.0 copy-start.3
  17.4 0.0 copy-start.4
  17.4 3.5 %planes.1 = f32[32,2,128]{2,1,0:T(2,128)S(1)} custom-call(f32[32,2,128]{2,1,0:T(2,128)S(1)} %all-to-all-done.columns_ref, f32[192,256]{1,0:T(8,128)S(1)} %get-tuple-element.7.x_ref, bf16[512,512]{1,0:T(8,128)(2,1)S(1)} %get-tuple-element.8.plus_ref, f32[12,192,192]{2,1,0:T(8,128)S(1)} %copy-done.5), custom_call_target="tpu_custom_call" | custom-call | flops 1811939328 | bytes 1835008 | tf_op jit(solution)/shard_map/planes/pallas_call | solution.py:382
  20.9 9.0 %all_to_all.10.columns_ref = f32[32,2,128]{2,1,0:T(2,128)S(1)} all-to-all(f32[32,2,128]{2,1,0:T(2,128)S(1)} %planes.1), channel_id=1, replica_groups=mesh['ga'=16,'band'=2] {'ga','band'}, dimensions={0} | all-to-all | bytes 65536 | tf_op jit(solution)/shard_map/all_to_all | solution.py:401
  29.9 0.0 copy-done
  29.9 0.0 copy-done.1
  29.9 0.0 copy-done.2
  29.9 0.0 copy-done.3
  30.0 0.0 copy-done.4
  30.0 2.0 %finish.1 = f32[2,2,4,192]{3,2,1,0:T(4,128)} custom-call(s32[1,16]{1,0:T(1,128)S(1)} %bitcast.9, f32[32,2,128]{2,1,0:T(2,128)S(1)} %all_to_all.10.columns_ref, s32[1,512]{1,0:T(1,128)S(1)} %bitcast.8, f32[512,512]{1,0:T(8,128)S(1)} %copy-done.1, bf16[1536,512]{1,0:T(8,128)(2,1)S(1)} %bitcast.7, bf16[2,2,192,512]{3,2,1,0:T(8,128)(2,1)S(1)} %copy-done.2), custom_call_target="tpu_custom_call" | custom-call | flops 41943040 | bytes 3420160 | tf_op jit(solution)/shard_map/finish/pallas_call | solution.py:404
Async XLA Ops:
  0.0 10.1 %copy-start.6 = (s32[128]{0:T(128)S(1)}, s32[128]{0:T(128)}, u32[]{:S(2)}) copy-start(s32[128]{0:T(128)} %param.13) | copy-start | bytes 1540
  2.7 14.6 %all-to-all-start = ((f32[32,2,128]{2,1,0:T(2,128)}), f32[32,2,128]{2,1,0:T(2,128)S(1)}, u32[]{:S(2)}, u32[]{:S(2)}) async-start(f32[32,2,128]{2,1,0:T(2,128)} %project.1), calls=%async_computation | async-start | bytes 65536 | tf_op jit(solution)/shard_map/all_to_all | solution.py:363
  10.1 7.3 %copy-start.5 = (f32[12,192,192]{2,1,0:T(8,128)S(1)}, f32[12,192,192]{2,1,0:T(8,128)}, u32[]{:S(2)}) copy-start(f32[12,192,192]{2,1,0:T(8,128)} %potential_ref.1) | copy-start | bytes 5308420
  17.4 12.5 %copy-start = (bf16[512,2,4,192]{0,3,2,1:T(8,128)(2,1)S(1)}, bf16[512,2,4,192]{0,3,2,1:T(8,128)(2,1)}, u32[]{:S(2)}) copy-start(bf16[512,2,4,192]{0,3,2,1:T(8,128)(2,1)} %param.9) | copy-start | bytes 4718596
  17.4 12.5 %copy-start.1 = (f32[512,512]{1,0:T(8,128)S(1)}, f32[512,512]{1,0:T(8,128)}, u32[]{:S(2)}) copy-start(f32[512,512]{1,0:T(8,128)} %couplings_ref.1) | copy-start | bytes 3145732
  17.4 12.5 %copy-start.2 = (bf16[2,2,192,512]{3,2,1,0:T(8,128)(2,1)S(1)}, bf16[2,2,192,512]{3,2,1,0:T(8,128)(2,1)}, u32[]{:S(2)}) copy-start(bf16[2,2,192,512]{3,2,1,0:T(8,128)(2,1)} %constant.2.clone.table_ref) | copy-start | bytes 2359300
  17.4 12.5 %copy-start.3 = (s32[512]{0:T(512)S(1)}, s32[512]{0:T(512)}, u32[]{:S(2)}) copy-start(s32[512]{0:T(512)} %param.12) | copy-start | bytes 6148
  17.4 12.5 %copy-start.4 = (s32[16]{0:T(128)S(1)}, s32[16]{0:T(128)}, u32[]{:S(2)}) copy-start(s32[16]{0:T(128)} %count_hbm.1) | copy-start | bytes 196
